TPU v7x, 128 devices: a whole 4x4x4 slice. The times are simulated.
128 devices in a mesh: dp: 32 (over y, z, core), ctx: 4 (over x).
Axes of the slice: x: 4, y: 4, z: 4, core: 2. Of those that a mesh axis runs over, the one named last changes fastest.
Arguments:
- tokens: bfloat16 [32, 1024, 4096], P('dp', 'ctx'), may hold values from -40.5 to 40.5
- doc_ids: int32 [32, 1024], P('dp', 'ctx'), may hold values from 0 to 5, never falling along the last dimension, each value on 1 to 512 neighbouring positions
- destinations: int32 [32], replicated, may hold values from 0 to 31, as said below
- norm_gain: float32 [4096], replicated, may hold values from 0.1 to 1.9
- w_query: bfloat16 [4096, 4096], P(None, 'ctx'), may hold values from -1 to 1
- w_key: bfloat16 [4096, 1024], P(None, 'ctx'), may hold values from -1 to 1
- w_value: bfloat16 [4096, 1024], P(None, 'ctx'), may hold values from -0.09375 to 0.09375
- w_out: bfloat16 [4096, 4096], P('ctx'), may hold values from -0.09375 to 0.09375
Outputs:
- attended: bfloat16 [32, 1024, 4096], P('dp', 'ctx')
- kv_cache: bfloat16 [32, 1024, 2048], P('dp', None, 'ctx')
Inputs may be any that keep to these rules, and one draw needn't show every extreme that they name: `doc_ids`: within a packed row the document numbers never fall; a document covers 1 to 512 positions, and some document covers exactly 512. destinations is a permutation of the groups made by sections b = 0, 1, ... up to log2 32 - 1 in order: in section b the two groups whose indices differ only in bit b either exchange the rows they hold or keep them. So before section b a row with anchor g sits at the group whose bits below b are those of destinations[g] and whose other bits are those of g.
All inputs are finite; a program needn't handle non-finite values.
Results may differ from a plain program's by a relative error of at most 0.0083.
Values may be sent and summed in bfloat16 or wider, within the bound.
No kernel may reach another device: no remote copies, remote signals or barrier semaphores. Data moves between devices by JAX's collectives and lax.ppermute only.
A program may use at most 128 MiB of HBM per device.

v0:
```python
import math

import jax
import jax.numpy as jnp
from jax import lax
from jax.sharding import PartitionSpec as P

HD = 128


def swapped(value, axis, apart):
    mask = 2**apart
    pairs = [(source, source ^ mask) for source in range(lax.axis_size(axis))]
    return lax.ppermute(value, axis, pairs)


def positions_of(doc_numbers):
    length = doc_numbers.shape[-1]
    row_index = jnp.arange(length, dtype=jnp.int32)
    same_doc = doc_numbers[..., :, None] == doc_numbers[..., None, :]
    doc_start = jnp.min(jnp.where(same_doc, row_index, length), axis=-1)
    return (row_index - doc_start).astype(jnp.float32)


def rotate(columns, positions):
    half_dim = columns.shape[-1] // 2
    inverse = 500000.0 ** (-2.0 * jnp.arange(half_dim, dtype=jnp.float32) / columns.shape[-1])
    angles = positions[..., None, None] * inverse
    cosine = jnp.cos(angles)
    sine_part = jnp.sin(angles)
    first_half = columns[..., :half_dim]
    second_half = columns[..., half_dim:]
    return jnp.concatenate(
        [
            first_half * cosine - second_half * sine_part,
            second_half * cosine + first_half * sine_part,
        ],
        axis=-1,
    )


def section_takes(destinations, bit_count):
    own_group = lax.axis_index("dp")
    anchors = jnp.arange(destinations.shape[0], dtype=jnp.int32)
    takes = []
    for bit in range(bit_count):
        low_mask = (1 << bit) - 1
        before = jnp.bitwise_and(destinations, low_mask) + (
            anchors - jnp.bitwise_and(anchors, low_mask)
        )
        moving = jnp.bitwise_and(jnp.right_shift(destinations, bit), 1) != jnp.bitwise_and(
            jnp.right_shift(own_group, bit), 1
        )
        takes.append(jnp.any((before == own_group) & moving))
    return takes


def attention_layer(rows_local, ids_local, norm_gain, w_query, w_key, w_value, w_out):
    whole_rows, whole_ids = (
        lax.all_gather(rows_local[None], "ctx", axis=0, tiled=True),
        lax.all_gather(ids_local[None], "ctx", axis=0, tiled=True),
    )
    ctx_count, pack_count, shard_rows, model_width = whole_rows.shape
    length = ctx_count * shard_rows
    local_heads = w_query.shape[1] // HD
    local_kv = w_key.shape[1] // HD
    group_size = local_heads // local_kv
    score_scale = 1.0 / math.sqrt(HD)
    seq_rows = whole_rows.transpose(1, 0, 2, 3).reshape(pack_count * length, model_width)
    seq_ids = whole_ids.transpose(1, 0, 2).reshape(pack_count, length)
    flat_rows = seq_rows.astype(jnp.float32)
    normed = (
        flat_rows
        * lax.rsqrt(jnp.mean(flat_rows * flat_rows, axis=-1, keepdims=True) + 1e-05)
        * norm_gain
    ).astype(jnp.bfloat16)
    positions = positions_of(seq_ids)
    queries = jnp.dot(normed, w_query, preferred_element_type=jnp.float32).reshape(
        pack_count, length, local_heads, HD
    )
    queries = rotate(queries, positions).astype(jnp.bfloat16)
    queries = queries.reshape(pack_count, length, local_kv, group_size, HD)
    rotated_keys = jnp.dot(normed, w_key, preferred_element_type=jnp.float32).reshape(
        pack_count, length, local_kv, HD
    )
    rotated_keys = rotate(rotated_keys, positions).astype(jnp.bfloat16)
    values = jnp.dot(normed, w_value, preferred_element_type=jnp.float32).astype(jnp.bfloat16)
    values = values.reshape(pack_count, length, local_kv, HD)
    row_index = jnp.arange(length, dtype=jnp.int32)
    causal = row_index[None, :] <= row_index[:, None]
    allowed = (causal[None] & (seq_ids[:, :, None] == seq_ids[:, None, :]))[:, None]

    def one_head(inputs):
        head_queries, head_keys, head_values = inputs
        scores = (
            jnp.einsum(
                "nigd,njd->ngij", head_queries, head_keys, preferred_element_type=jnp.float32
            )
            * score_scale
        )
        scores = jnp.where(allowed, scores, -1e30)
        row_max = jnp.max(scores, axis=-1, keepdims=True)
        exp_scores = jnp.exp(scores - row_max)
        attn_weights = (exp_scores / jnp.sum(exp_scores, axis=-1, keepdims=True)).astype(
            jnp.bfloat16
        )
        context = jnp.einsum(
            "ngij,njd->nigd", attn_weights, head_values, preferred_element_type=jnp.float32
        )
        return context.astype(jnp.bfloat16)

    per_head = lax.map(
        one_head,
        (
            queries.transpose(2, 0, 1, 3, 4),
            rotated_keys.transpose(2, 0, 1, 3),
            values.transpose(2, 0, 1, 3),
        ),
    )
    context = per_head.transpose(1, 2, 0, 3, 4).reshape(
        pack_count, ctx_count, shard_rows, local_heads * HD
    )
    context = context.transpose(1, 0, 2, 3).reshape(
        ctx_count * pack_count * shard_rows, local_heads * HD
    )
    attended = lax.psum_scatter(
        jnp.dot(context, w_out, preferred_element_type=jnp.float32),
        "ctx",
        scatter_dimension=0,
        tiled=True,
    )
    attended = attended.astype(jnp.bfloat16).reshape(pack_count, shard_rows, model_width)
    kv_block = jnp.stack([rotated_keys, values], axis=3).reshape(
        pack_count, length, local_kv * 2 * HD
    )
    return (attended, kv_block)


def shards(tokens, doc_ids, destinations, norm_gain, w_query, w_key, w_value, w_out):
    bit_count = lax.axis_size("dp").bit_length() - 1
    takes = section_takes(destinations, bit_count)
    rows, ids = (tokens, doc_ids)
    for bit in range(bit_count):
        moved_rows, moved_ids = swapped((rows, ids), "dp", bit)
        rows = jnp.where(takes[bit], moved_rows, rows)
        ids = jnp.where(takes[bit], moved_ids, ids)
    attended, kv_cache = attention_layer(rows, ids, norm_gain, w_query, w_key, w_value, w_out)
    for bit in reversed(range(bit_count)):
        moved_back = swapped(attended, "dp", bit)
        attended = jnp.where(takes[bit], moved_back, attended)
    return (attended, kv_cache)


def solution(mesh):
    return jax.shard_map(
        shards,
        mesh=mesh,
        in_specs=(
            P("dp", "ctx", None),
            P("dp", "ctx"),
            P(),
            P(),
            P(None, "ctx"),
            P(None, "ctx"),
            P(None, "ctx"),
            P("ctx", None),
        ),
        out_specs=(P("dp", "ctx", None), P("dp", None, "ctx")),
        check_vma=False,
    )
```

profile of v0, /device:TPU:1, one launch (start us, length us, event | category | flops | bytes accessed | tf_op | source)
XLA Modules:
  0.0 748.2 jit_solution(13894116149539495917)
XLA Ops:
  17.1 45.7 %collective-permute-done.1 = bf16[1,256,4096]{2,1,0:T(8,128)(2,1)S(1)} collective-permute-done((bf16[1,256,4096]{2,1,0:T(8,128)(2,1)S(1)}, bf16[1,256,4096]{2,1,0:T(8,128)(2,1)S(1)}, u32[]{:S(2)}, u32[]{:S(2)}) %collective-permute-start.1) | collective-permute-done | bytes 2097184 | tf_op jit(solution)/shard_map/ppermute | solution.py:14
  66.8 44.8 %collective-permute-done.2 = bf16[1,256,4096]{2,1,0:T(8,128)(2,1)S(1)} collective-permute-done((bf16[1,256,4096]{2,1,0:T(8,128)(2,1)S(1)}, bf16[1,256,4096]{2,1,0:T(8,128)(2,1)S(1)}, u32[]{:S(2)}, u32[]{:S(2)}) %collective-permute-start.2) | collective-permute-done | bytes 2097184 | tf_op jit(solution)/shard_map/ppermute | solution.py:14
  113.8 44.0 %collective-permute-done.3 = bf16[1,256,4096]{2,1,0:T(8,128)(2,1)S(1)} collective-permute-done((bf16[1,256,4096]{2,1,0:T(8,128)(2,1)S(1)}, bf16[1,256,4096]{2,1,0:T(8,128)(2,1)S(1)}, u32[]{:S(2)}, u32[]{:S(2)}) %collective-permute-start.3) | collective-permute-done | bytes 2097184 | tf_op jit(solution)/shard_map/ppermute | solution.py:14
  161.7 43.0 %collective-permute-done.4 = bf16[1,256,4096]{2,1,0:T(8,128)(2,1)S(1)} collective-permute-done((bf16[1,256,4096]{2,1,0:T(8,128)(2,1)S(1)}, bf16[1,256,4096]{2,1,0:T(8,128)(2,1)S(1)}, u32[]{:S(2)}, u32[]{:S(2)}) %collective-permute-start.4) | collective-permute-done | bytes 2097184 | tf_op jit(solution)/shard_map/ppermute | solution.py:14
  230.7 11.8 %copy.46 = bf16[1024,4096]{1,0:T(8,128)(2,1)} copy(bf16[1024,4096]{0,1:T(8,128)(2,1)} %bitcast.132) | data formatting | bytes 16777216 | tf_op jit(solution)/shard_map/dot_general | solution.py:78
  243.2 8.8 %all-gather.2 = s32[4,1,256]{2,1,0:T(1,128)S(1)} all-gather(s32[1,1,256]{2,1,0:T(1,128)S(1)} %fusion.31), channel_id=3, replica_groups=mesh['dp'=32,'ctx'=4] {'ctx'}, dimensions={0}, use_global_device_ids=true | all-gather | bytes 5120 | tf_op jit(solution)/shard_map/all_gather | solution.py:61
  253.8 40.4 %all-gather.5.cloned.1.call-done = bf16[4,256,4096]{2,1,0:T(8,128)(2,1)} async-done(((bf16[1,256,4096]{2,1,0:T(8,128)(2,1)}), bf16[4,256,4096]{2,1,0:T(8,128)(2,1)}) %all-gather.5.cloned.1.call-update) | async-done | bytes 8388624 | tf_op jit(solution)/shard_map/all_gather | solution.py:60
  294.3 5.2 multiply_reduce_fusion
  300.0 4.6 convolution_bitcast_fusion.1
  304.7 9.0 %convolution_bitcast_fusion = f32[1,1024,8,128]{1,3,2,0:T(8,128)S(1)} fusion(bf16[8,128,4096]{2,1,0:T(8,128)(2,1)S(1)} %bitcast.135, f32[4096]{0:T(1024)S(1)} %copy-done.12, f32[1024]{0:T(1024)S(1)} %bitcast.148, bf16[1024,1,1,1,4096]{4,0,3,2,1:T(8,128)(2,1)S(1)} %bitcast.131), kind=kOutput, calls=%fused_computation.32 | convolution fusion | flops 8606711808 | bytes 20992000 | tf_op jit(solution)/shard_map/dot_general | solution.py:78
  322.2 10.4 %fusion.29 = bf16[1024,4096]{1,0:T(8,128)(2,1)} fusion(f32[4096]{0:T(1024)S(1)} %copy-done.12, f32[1024]{0:T(1024)S(1)} %bitcast.149, bf16[4,256,4096]{2,1,0:T(8,128)(2,1)} %all-gather.5.cloned.1.call-done), kind=kLoop, calls=%fused_computation.27 | loop fusion | flops 16777216 | bytes 16797696 | tf_op jit(solution)/shard_map/convert_element_type | solution.py:76
  332.6 5.9 convolution_convert_fusion
  341.1 31.3 %while.11 = (s32[]{:T(128)}, bf16[2,1,1024,4,128]{2,4,3,1,0:T(8,128)(2,1)}, bf16[2,1,1024,128]{2,3,1,0:T(8,128)(2,1)S(1)}, bf16[2,1,1024,128]{2,3,0,1:T(8,128)(2...) while((s32[]{:T(128)}, ...), condition=%wide.region_10.11_spmd.clone, body=%wide.region_7.10_spmd.clone.sunk | while | flops 2201477120 | bytes 74012808 | solution.py:112
  341.9 4.4 fusion.56
  350.0 5.5 fusion.58
  357.4 4.4 fusion.56
  365.5 5.5 fusion.58
  372.3 16.2 %fusion.40 = f32[1024,4096]{1,0:T(8,128)} fusion(bf16[1024,1024]{0,1:T(8,128)(2,1)} %bitcast.150, bf16[1024,4096]{1,0:T(8,128)(2,1)} %param.17), kind=kOutput, calls=%fused_computation.79 | convolution fusion | flops 8589934592 | bytes 27262976 | tf_op jit(solution)/shard_map/dot_general | solution.py:127
  388.5 149.1 %reduce-scatter.2.cloned.1.call-done = f32[256,4096]{1,0:T(8,128)} async-done(((f32[1024,4096]{1,0:T(8,128)}), f32[256,4096]{1,0:T(8,128)}) %reduce-scatter.2.cloned.1.call-update) | async-done | bytes 4194320 | tf_op jit(solution)/shard_map/reduce_scatter | solution.py:126
  543.0 45.3 %collective-permute-done.10 = bf16[1,256,4096]{2,1,0:T(8,128)(2,1)S(1)} collective-permute-done((bf16[1,256,4096]{2,1,0:T(8,128)(2,1)S(1)}, bf16[1,256,4096]{2,1,0:T(8,128)(2,1)S(1)}, u32[]{:S(2)}, u32[]{:S(2)}) %collective-permute-start.10) | collective-permute-done | bytes 2097184 | tf_op jit(solution)/shard_map/ppermute | solution.py:14
  590.5 44.4 %collective-permute-done.11 = bf16[1,256,4096]{2,1,0:T(8,128)(2,1)S(1)} collective-permute-done((bf16[1,256,4096]{2,1,0:T(8,128)(2,1)S(1)}, bf16[1,256,4096]{2,1,0:T(8,128)(2,1)S(1)}, u32[]{:S(2)}, u32[]{:S(2)}) %collective-permute-start.11) | collective-permute-done | bytes 2097184 | tf_op jit(solution)/shard_map/ppermute | solution.py:14
  638.7 43.4 %collective-permute-done.12 = bf16[1,256,4096]{2,1,0:T(8,128)(2,1)S(1)} collective-permute-done((bf16[1,256,4096]{2,1,0:T(8,128)(2,1)S(1)}, bf16[1,256,4096]{2,1,0:T(8,128)(2,1)S(1)}, u32[]{:S(2)}, u32[]{:S(2)}) %collective-permute-start.12) | collective-permute-done | bytes 2097184 | tf_op jit(solution)/shard_map/ppermute | solution.py:14
  684.4 42.5 %collective-permute-done.13 = bf16[1,256,4096]{2,1,0:T(8,128)(2,1)S(1)} collective-permute-done((bf16[1,256,4096]{2,1,0:T(8,128)(2,1)S(1)}, bf16[1,256,4096]{2,1,0:T(8,128)(2,1)S(1)}, u32[]{:S(2)}, u32[]{:S(2)}) %collective-permute-start.13) | collective-permute-done | bytes 2097184 | tf_op jit(solution)/shard_map/ppermute | solution.py:14
  728.9 4.3 collective-permute-start.14
  (104 shorter events, 94.8 us)
Async XLA Ops:
  7.2 325.4 %copy-start = (bf16[4096,256]{1,0:T(8,128)(2,1)S(1)}, bf16[4096,256]{1,0:T(8,128)(2,1)}, u32[]{:S(2)}) copy-start(bf16[4096,256]{1,0:T(8,128)(2,1)} %param.16) | copy-start | bytes 6291460
  7.2 287.1 %all-gather.5.cloned.1.call-start = ((), (), s32[]{:S(2)}) async-start(), calls=%async_computation.2 | async-start | bytes 10485760 | tf_op jit(solution)/shard_map/all_gather | solution.py:60
  7.2 5.6 collective-permute-start
  15.3 47.5 %collective-permute-start.1 = (bf16[1,256,4096]{2,1,0:T(8,128)(2,1)S(1)}, bf16[1,256,4096]{2,1,0:T(8,128)(2,1)S(1)}, u32[]{:S(2)}, u32[]{:S(2)}) collective-permute-start(bf16[1,256,4096]{2,1,0:T(8,128)(2,1)S(1)} %broadcast_select_fusion.9), channel_id=1, source_target_pairs={{0,8},{4,12},{8,0},{12,4},{16,24},{20,28},{24,16},{28,20},{32,40},... | collective-permute-start | bytes 6291464 | tf_op jit(solution)/shard_map/ppermute | solution.py:14
  63.6 48.0 %collective-permute-start.2 = (bf16[1,256,4096]{2,1,0:T(8,128)(2,1)S(1)}, bf16[1,256,4096]{2,1,0:T(8,128)(2,1)S(1)}, u32[]{:S(2)}, u32[]{:S(2)}) collective-permute-start(bf16[1,256,4096]{2,1,0:T(8,128)(2,1)S(1)} %broadcast_select_fusion.7), channel_id=1, source_target_pairs={{0,16},{4,20},{8,24},{12,28},{16,0},{20,4},{24,8},{28,12},{32,48},... | collective-permute-start | bytes 6291464 | tf_op jit(solution)/shard_map/ppermute | solution.py:14
  112.4 45.4 %collective-permute-start.3 = (bf16[1,256,4096]{2,1,0:T(8,128)(2,1)S(1)}, bf16[1,256,4096]{2,1,0:T(8,128)(2,1)S(1)}, u32[]{:S(2)}, u32[]{:S(2)}) collective-permute-start(bf16[1,256,4096]{2,1,0:T(8,128)(2,1)S(1)} %broadcast_select_fusion.5), channel_id=1, source_target_pairs={{0,32},{4,36},{8,40},{12,44},{16,48},{20,52},{24,56},{28,60},{32,0... | collective-permute-start | bytes 6291464 | tf_op jit(solution)/shard_map/ppermute | solution.py:14
  158.7 46.0 %collective-permute-start.4 = (bf16[1,256,4096]{2,1,0:T(8,128)(2,1)S(1)}, bf16[1,256,4096]{2,1,0:T(8,128)(2,1)S(1)}, u32[]{:S(2)}, u32[]{:S(2)}) collective-permute-start(bf16[1,256,4096]{2,1,0:T(8,128)(2,1)S(1)} %broadcast_select_fusion.3), channel_id=1, source_target_pairs={{0,64},{4,68},{8,72},{12,76},{16,80},{20,84},{24,88},{28,92},{32,9... | collective-permute-start | bytes 6291464 | tf_op jit(solution)/shard_map/ppermute | solution.py:14
  206.9 330.7 %reduce-scatter.2.cloned.1.call-start = ((), (), s32[]{:S(2)}) async-start(), calls=%async_computation.1 | async-start | bytes 20971520 | tf_op jit(solution)/shard_map/reduce_scatter | solution.py:126
  207.5 4.5 collective-permute-start.5
  212.6 2.5 collective-permute-start.6
  215.7 4.0 collective-permute-start.7
  220.4 2.5 collective-permute-start.8
  223.6 19.0 %collective-permute-start.9 = (s32[1,256]{1,0:T(1,128)S(1)}, s32[1,256]{1,0:T(1,128)S(1)}, u32[]{:S(2)}, u32[]{:S(2)}) collective-permute-start(s32[1,256]{1,0:T(1,128)S(1)} %broadcast_select_fusion.13), channel_id=1, source_target_pairs={{0,64},{4,68},{8,72},{12,76},{16,80},{20,84},{24,88},{28,92},{32,9... | collective-permute-start | bytes 3080 | tf_op jit(solution)/shard_map/ppermute | solution.py:14
  253.8 60.0 %copy-start.10 = (f32[1024,64]{0,1:T(8,128)}, f32[1024,64]{0,1:T(8,128)S(1)}, u32[]{:S(2)}) copy-start(f32[1024,64]{0,1:T(8,128)S(1)} %get-tuple-element.103) | copy-start | bytes 786436
  253.8 60.0 %copy-start.11 = (f32[1024,64]{0,1:T(8,128)}, f32[1024,64]{0,1:T(8,128)S(1)}, u32[]{:S(2)}) copy-start(f32[1024,64]{0,1:T(8,128)S(1)} %get-tuple-element.104) | copy-start | bytes 786436
  253.8 45.7 %copy-start.12 = (f32[4096]{0:T(1024)S(1)}, f32[4096]{0:T(1024)}, u32[]{:S(2)}) copy-start(f32[4096]{0:T(1024)} %param.13) | copy-start | bytes 49156
  537.6 50.8 %copy-start.3 = (f32[256,4096]{1,0:T(8,128)S(1)}, f32[256,4096]{1,0:T(8,128)}, u32[]{:S(2)}) copy-start(f32[256,4096]{1,0:T(8,128)} %reduce-scatter.2.cloned.1.call-done) | copy-start | bytes 12582916
  540.2 48.1 %collective-permute-start.10 = (bf16[1,256,4096]{2,1,0:T(8,128)(2,1)S(1)}, bf16[1,256,4096]{2,1,0:T(8,128)(2,1)S(1)}, u32[]{:S(2)}, u32[]{:S(2)}) collective-permute-start(bf16[1,256,4096]{2,1,0:T(8,128)(2,1)S(1)} %convert_bitcast_fusion), channel_id=1, source_target_pairs={{0,64},{4,68},{8,72},{12,76},{16,80},{20,84},{24,88},{28,92},{32,9... | collective-permute-start | bytes 6291464 | tf_op jit(solution)/shard_map/ppermute | solution.py:14
  589.2 45.7 %collective-permute-start.11 = (bf16[1,256,4096]{2,1,0:T(8,128)(2,1)S(1)}, bf16[1,256,4096]{2,1,0:T(8,128)(2,1)S(1)}, u32[]{:S(2)}, u32[]{:S(2)}) collective-permute-start(bf16[1,256,4096]{2,1,0:T(8,128)(2,1)S(1)} %broadcast_select_fusion), channel_id=1, source_target_pairs={{0,32},{4,36},{8,40},{12,44},{16,48},{20,52},{24,56},{28,60},{32,0... | collective-permute-start | bytes 6291464 | tf_op jit(solution)/shard_map/ppermute | solution.py:14
  635.8 46.3 %collective-permute-start.12 = (bf16[1,256,4096]{2,1,0:T(8,128)(2,1)S(1)}, bf16[1,256,4096]{2,1,0:T(8,128)(2,1)S(1)}, u32[]{:S(2)}, u32[]{:S(2)}) collective-permute-start(bf16[1,256,4096]{2,1,0:T(8,128)(2,1)S(1)} %broadcast_select_fusion.2), channel_id=1, source_target_pairs={{0,16},{4,20},{8,24},{12,28},{16,0},{20,4},{24,8},{28,12},{32,48},... | collective-permute-start | bytes 6291464 | tf_op jit(solution)/shard_map/ppermute | solution.py:14
  683.0 50.2 %copy-start.7 = (bf16[1,1024,2,64]{1,3,2,0:T(8,128)(2,1)S(1)}, bf16[1,1024,2,64]{1,3,2,0:T(8,128)(2,1)}, u32[]{:S(2)}) copy-start(bf16[1,1024,2,64]{1,3,2,0:T(8,128)(2,1)} %copy-done.6) | copy-start | bytes 786436
  683.0 50.2 %copy-start.9 = (bf16[1,1024,2,64]{1,3,2,0:T(8,128)(2,1)S(1)}, bf16[1,1024,2,64]{1,3,2,0:T(8,128)(2,1)}, u32[]{:S(2)}) copy-start(bf16[1,1024,2,64]{1,3,2,0:T(8,128)(2,1)} %get-tuple-element.102) | copy-start | bytes 786436
  683.0 43.9 %collective-permute-start.13 = (bf16[1,256,4096]{2,1,0:T(8,128)(2,1)S(1)}, bf16[1,256,4096]{2,1,0:T(8,128)(2,1)S(1)}, u32[]{:S(2)}, u32[]{:S(2)}) collective-permute-start(bf16[1,256,4096]{2,1,0:T(8,128)(2,1)S(1)} %broadcast_select_fusion.4), channel_id=1, source_target_pairs={{0,8},{4,12},{8,0},{12,4},{16,24},{20,28},{24,16},{28,20},{32,40},... | collective-permute-start | bytes 6291464 | tf_op jit(solution)/shard_map/ppermute | solution.py:14
  728.9 8.4 %collective-permute-start.14 = (bf16[1,256,4096]{2,1,0:T(8,128)(2,1)}, bf16[1,256,4096]{2,1,0:T(8,128)(2,1)}, u32[]{:S(2)}, u32[]{:S(2)}) collective-permute-start(bf16[1,256,4096]{2,1,0:T(8,128)(2,1)} %broadcast_select_fusion.6), channel_id=1, source_target_pairs={{0,4},{4,0},{8,12},{12,8},{16,20},{20,16},{24,28},{28,24},{32,36},... | collective-permute-start | bytes 6291464 | tf_op jit(solution)/shard_map/ppermute | solution.py:14
  (13 other events, 81.0 us)
Sparse Core Ops, SparseCore 0:
  207.0 87.2 all-gather.4
  388.6 148.8 reduce-scatter.1
where the time goes:
time: 753 us; the launch traced here: 748 us
  waiting for transfers between devices  553 us (73%)
  matrix products  55.5 us (7%)
  other arithmetic  55.2 us (7%)
  starting transfers between devices  34.6 us (5%)
  local copies, waits for them, and re-layouts  25.8 us (3%)
  between operations  14.6 us (2%)
  blocking collectives  8.81 us (1%)
    ppermute x15, waiting for transfers between devices, swapped(): return lax.ppermute(value, axis, pairs)  364 us
    reduce_scatter x1, waiting for transfers between devices, attention_layer(): lax.psum_scatter(jnp.dot(context, w_out, preferred_element_type=jnp.float...  149 us
    all_gather x1, waiting for transfers between devices, attention_layer(): lax.all_gather(rows_local[None], 'ctx', axis=0, tiled=True)  40.4 us
    ppermute x15, starting transfers between devices, swapped(): return lax.ppermute(value, axis, pairs)  34.5 us
    dot_general x1, matrix products, attention_layer(): jnp.dot(context, w_out, preferred_element_type=jnp.float32)  16.2 us
  transfers between devices with their start and end apart: 17, of which 16 were waited for; matrix products, arithmetic and copies ran while one was open for 3% of the time, Pallas kernels for 0%

commit v1 on v0

--- a/solution.py
+++ b/solution.py
@@ -6,12 +6,6 @@
 from jax.sharding import PartitionSpec as P
 
 HD = 128
-
-
-def swapped(value, axis, apart):
-    mask = 2**apart
-    pairs = [(source, source ^ mask) for source in range(lax.axis_size(axis))]
-    return lax.ppermute(value, axis, pairs)
 
 
 def positions_of(doc_numbers):
@@ -39,20 +33,14 @@
     )
 
 
-def section_takes(destinations, bit_count):
-    own_group = lax.axis_index("dp")
-    anchors = jnp.arange(destinations.shape[0], dtype=jnp.int32)
-    takes = []
-    for bit in range(bit_count):
-        low_mask = (1 << bit) - 1
-        before = jnp.bitwise_and(destinations, low_mask) + (
-            anchors - jnp.bitwise_and(anchors, low_mask)
-        )
-        moving = jnp.bitwise_and(jnp.right_shift(destinations, bit), 1) != jnp.bitwise_and(
-            jnp.right_shift(own_group, bit), 1
-        )
-        takes.append(jnp.any((before == own_group) & moving))
-    return takes
+def routed(block, destinations):
+    groups = lax.axis_size("dp")
+    anchors = jnp.arange(groups, dtype=jnp.int32)
+    source = jnp.sum(jnp.where(destinations[None, :] == anchors[:, None], anchors[None, :], 0), axis=1)
+    pieces = block.reshape(groups, block.shape[0] // groups, block.shape[1])
+    scattered = lax.all_to_all(pieces, "dp", 0, 0, tiled=False)
+    ordered = jnp.take(scattered, source, axis=0)
+    return lax.all_to_all(ordered, "dp", 0, 0, tiled=False).reshape(block.shape)
 
 
 def attention_layer(rows_local, ids_local, norm_gain, w_query, w_key, w_value, w_out):
@@ -137,18 +125,10 @@
 
 
 def shards(tokens, doc_ids, destinations, norm_gain, w_query, w_key, w_value, w_out):
-    bit_count = lax.axis_size("dp").bit_length() - 1
-    takes = section_takes(destinations, bit_count)
-    rows, ids = (tokens, doc_ids)
-    for bit in range(bit_count):
-        moved_rows, moved_ids = swapped((rows, ids), "dp", bit)
-        rows = jnp.where(takes[bit], moved_rows, rows)
-        ids = jnp.where(takes[bit], moved_ids, ids)
-    attended, kv_cache = attention_layer(rows, ids, norm_gain, w_query, w_key, w_value, w_out)
-    for bit in reversed(range(bit_count)):
-        moved_back = swapped(attended, "dp", bit)
-        attended = jnp.where(takes[bit], moved_back, attended)
-    return (attended, kv_cache)
+    attended, kv_block = attention_layer(
+        tokens, doc_ids, norm_gain, w_query, w_key, w_value, w_out
+    )
+    return (attended, routed(kv_block[0], destinations)[None])
 
 
 def solution(mesh):

time: 753 us -> 353 us (0.47)
  waiting for transfers between devices: 553 us -> 177 us
  starting transfers between devices: 34.6 us -> 7.85 us
  blocking collectives: 8.81 us -> 30.1 us
  other arithmetic: 55.2 us -> 39.6 us
    ppermute x15 -> x0, waiting for transfers between devices: 364 us -> none  [swapped(): return lax.ppermute(value, axis, pairs)]
    reduce_scatter x1, waiting for transfers between devices: 149 us -> 98.4 us  [attention_layer(): lax.psum_scatter(jnp.dot(context, w_out, preferred_element_type=jnp.float...]
    ppermute x15 -> x0, starting transfers between devices: 34.5 us -> none  [swapped(): return lax.ppermute(value, axis, pairs)]
    all_to_all x0 -> x1, blocking collectives: none -> 20.6 us  [routed(): return lax.all_to_all(ordered, 'dp', 0, 0, tiled=False).reshape(block.shape)]
    all_gather x1, waiting for transfers between devices: 40.4 us -> 61 us  [attention_layer(): lax.all_gather(rows_local[None], 'ctx', axis=0, tiled=True)]
    select_n x14 -> x2, other arithmetic: 18.2 us -> 0.17 us  [routed(): ordered = jnp.take(scattered, source, axis=0)]
    all_to_all x0 -> x1, waiting for transfers between devices: none -> 16.8 us  [routed(): scattered = lax.all_to_all(pieces, 'dp', 0, 0, tiled=False)]
    all_to_all x0 -> x1, starting transfers between devices: none -> 7.77 us  [routed(): scattered = lax.all_to_all(pieces, 'dp', 0, 0, tiled=False)]
  transfers between devices with their start and end apart: 17 -> 3, of which waited for: 16 -> 3; matrix products, arithmetic and copies ran while one was open for 3% -> 6% of each run, Pallas kernels for 0% -> 0%
where the time goes in v1:
time: 353 us; the launch traced here: 352 us
  waiting for transfers between devices  177 us (50%)
  matrix products  56.8 us (16%)
  other arithmetic  39.6 us (11%)
  blocking collectives  30.1 us (9%)
  local copies, waits for them, and re-layouts  26.8 us (8%)
  between operations  14.3 us (4%)
  starting transfers between devices  7.85 us (2%)
    reduce_scatter x1, waiting for transfers between devices, attention_layer(): lax.psum_scatter(jnp.dot(context, w_out, preferred_element_type=jnp.float...  98.4 us
    all_gather x1, waiting for transfers between devices, attention_layer(): lax.all_gather(rows_local[None], 'ctx', axis=0, tiled=True)  61 us
    all_to_all x1, blocking collectives, routed(): return lax.all_to_all(ordered, 'dp', 0, 0, tiled=False).reshape(block.shape)  20.6 us
    all_to_all x1, waiting for transfers between devices, routed(): scattered = lax.all_to_all(pieces, 'dp', 0, 0, tiled=False)  16.8 us
    dot_general x1, matrix products, attention_layer(): jnp.dot(context, w_out, preferred_element_type=jnp.float32)  16.1 us
    dot_general x2, matrix products, one_head(): jnp.einsum('ngij,njd->nigd', attn_weights, head_values, preferred_element...  12.4 us
    dot_general x1, local copies, waits for them, and re-layouts, attention_layer(): jnp.dot(normed, w_query, preferred_element_type=jnp.float32)  11.6 us
    convert_element_type x1, other arithmetic, attention_layer(): normed = (flat_rows * lax.rsqrt(jnp.mean(flat_rows * flat_rows, axis=-1,...  10.4 us
  transfers between devices with their start and end apart: 3, of which 3 were waited for; matrix products, arithmetic and copies ran while one was open for 6% of the time, Pallas kernels for 0%

profile of v1, /device:TPU:1, one launch (start us, length us, event | category | flops | bytes accessed | tf_op | source)
XLA Modules:
  0.0 352.4 jit_solution(14745451803145040736)
XLA Ops:
  8.0 4.2 %copy.42 = bf16[256,4096]{1,0:T(8,128)(2,1)} copy(bf16[256,4096]{0,1:T(8,128)(2,1)} %bitcast.142) | data formatting | bytes 4194304 | tf_op jit(solution)/shard_map/dot_general | solution.py:71
  12.1 11.6 %copy.43 = bf16[1024,4096]{1,0:T(8,128)(2,1)} copy(bf16[1024,4096]{0,1:T(8,128)(2,1)} %bitcast.133) | data formatting | bytes 16777216 | tf_op jit(solution)/shard_map/dot_general | solution.py:66
  23.8 9.5 %all-gather.2 = s32[4,1,256]{2,1,0:T(1,128)S(1)} all-gather(s32[1,1,256]{2,1,0:T(1,128)S(1)} %bitcast.151), channel_id=3, replica_groups=mesh['dp'=32,'ctx'=4] {'ctx'}, dimensions={0}, use_global_device_ids=true | all-gather | bytes 5120 | tf_op jit(solution)/shard_map/all_gather | solution.py:49
  35.0 61.0 %all-gather.5.cloned.1.call-done = bf16[4,256,4096]{2,1,0:T(8,128)(2,1)} async-done(((bf16[1,256,4096]{2,1,0:T(8,128)(2,1)}), bf16[4,256,4096]{2,1,0:T(8,128)(2,1)}) %all-gather.5.cloned.1.call-update) | async-done | bytes 8388624 | tf_op jit(solution)/shard_map/all_gather | solution.py:48
  96.0 5.2 %multiply_reduce_fusion = f32[4,256]{1,0:T(4,128)S(1)} fusion(bf16[4,256,4096]{2,1,0:T(8,128)(2,1)} %all-gather.5.cloned.1.call-done), kind=kLoop, calls=%fused_computation.29 | loop fusion | flops 12581888 | bytes 8392704 | tf_op jit(solution)/shard_map/reduce_sum | solution.py:62
  101.8 4.6 %convolution_bitcast_fusion.1 = f32[1,1024,2,128]{1,3,2,0:T(8,128)S(1)} fusion(bf16[2,128,4096]{2,1,0:T(8,128)(2,1)} %bitcast.143, f32[4096]{0:T(1024)S(1)} %copy-done.8, f32[1024]{0:T(1024)S(1)} %bitcast.148, bf16[1024,1,1,1,4096]{4,0,3,2,1:T(8,128)(2,1)S(1)} %bitcast.131), kind=kOutput, calls=%fused_computation.38 | convolution fusion | flops 2164260864 | bytes 11554816 | tf_op jit(solution)/shard_map/dot_general | solution.py:71
  106.5 9.0 %convolution_bitcast_fusion = f32[1,1024,8,128]{1,3,2,0:T(8,128)S(1)} fusion(bf16[8,128,4096]{2,1,0:T(8,128)(2,1)S(1)} %bitcast.136, f32[4096]{0:T(1024)S(1)} %copy-done.8, f32[1024]{0:T(1024)S(1)} %bitcast.149, bf16[1024,1,1,1,4096]{4,0,3,2,1:T(8,128)(2,1)S(1)} %bitcast.132), kind=kOutput, calls=%fused_computation.33 | convolution fusion | flops 8606711808 | bytes 20992000 | tf_op jit(solution)/shard_map/dot_general | solution.py:66
  116.4 2.9 subtract_convert_fusion
  124.9 4.7 %maximum_bitcast_fusion = bf16[2,1,1024,4,128]{4,2,3,1,0:T(8,128)(2,1)} fusion(bf16[1,1024,2,4,64]{4,1,3,0,2:T(8,128)(2,1)} %copy.38, bf16[1,1024,2,4,64]{4,1,3,0,2:T(8,128)(2,1)} %copy.37), kind=kLoop, calls=%fused_computation.34 | loop fusion | flops 4194304 | bytes 4194304 | tf_op jit(solution)/shard_map/transpose | solution.py:103
  129.6 10.4 %fusion.29 = bf16[1024,4096]{1,0:T(8,128)(2,1)} fusion(f32[4096]{0:T(1024)S(1)} %copy-done.8, f32[1024]{0:T(1024)S(1)} %bitcast.150, bf16[4,256,4096]{2,1,0:T(8,128)(2,1)} %all-gather.5.cloned.1.call-done), kind=kLoop, calls=%fused_computation.28 | loop fusion | flops 16777216 | bytes 16797696 | tf_op jit(solution)/shard_map/convert_element_type | solution.py:64
  140.0 5.7 %convolution_convert_fusion = bf16[1024,256]{0,1:T(8,128)(2,1)S(1)} fusion(bf16[1024,4096]{1,0:T(8,128)(2,1)} %fusion.29, bf16[4096,256]{1,0:T(8,128)(2,1)S(1)} %copy-done), kind=kOutput, calls=%fused_computation.39 | convolution fusion | flops 2147745792 | bytes 11010048 | tf_op jit(solution)/shard_map/dot_general | solution.py:75
  145.7 29.8 %while.11 = (s32[]{:T(128)}, bf16[2,1,1024,4,128]{2,4,3,1,0:T(8,128)(2,1)}, bf16[2,1,1024,128]{2,3,1,0:T(8,128)(2,1)S(1)}, bf16[2,1,1024,128]{2,3,0,1:T(8,128)(2...) while((s32[]{:T(128)}, ...), condition=%wide.region_5.6_spmd.clone, body=%wide.region_2.5_spmd.clone.sunk | while | flops 2201477120 | bytes 57235532 | solution.py:100
  146.3 4.4 %fusion.52 = (f32[4,1024]{1,0:T(4,128)S(1)}, f32[1024,1024,4]{1,0,2:T(8,128)S(1)}) fusion(pred[1024,1024]{0,1:T(8,128)(4,1)S(1)} %fusion.51, bf16[2,1,1024,4,128]{4,2,3,1,0:T(8,128)(2,1)} %get-tuple-element.153, s32[]{:T(128)} %get-tuple-element.142, bf16[2,1,1024,128]{2,3,0,1:T(8,128)(2,1)S(1)} %get-tuple-element.152), kind=kOutput, calls=%fused_computation.6.clone.1 | convolution fusion | flops 1086320640 | bytes 19153920 | tf_op jit(solution)/shard_map/while/body/eval_jaxpr/nigd,njd->ngij/dot_general | solution.py:84
  150.8 3.7 %fusion.53 = f32[4,1024]{1,0:T(4,128)S(1)} fusion(f32[1024,1024,4]{1,0,2:T(8,128)S(1)} %get-tuple-element.133, f32[4,1024]{1,0:T(4,128)S(1)} %get-tuple-element.134, pred[1024,1024]{0,1:T(8,128)(4,1)S(1)} %fusion.51), kind=kLoop, calls=%fused_computation.5.clone.1 | loop fusion | flops 16773120 | bytes 17858560 | tf_op jit(solution)/shard_map/while/body/eval_jaxpr/reduce_sum | solution.py:92
  154.4 6.2 %fusion.54 = bf16[2,1,1024,4,128]{2,4,3,1,0:T(8,128)(2,1)} fusion(bf16[2,1,1024,4,128]{2,4,3,1,0:T(8,128)(2,1)} %get-tuple-element.143, s32[]{:T(128)} %get-tuple-element.142, f32[4,1024]{1,0:T(4,128)S(1)} %fusion.53, f32[4,1024]{1,0:T(4,128)S(1)} %get-tuple-element.134, f32[1024,1024,4]{1,0,2:T(8,128)S(1)} %get-tuple-element.133, ...), kind=kOutput, calls=%fused_computation.14.clone.1 | convolution fusion | flops 1095237632 | bytes 19170304 | tf_op jit(solution)/shard_map/while/body/eval_jaxpr/ngij,njd->nigd/dot_general | solution.py:95
  161.2 4.4 %fusion.52 = (f32[4,1024]{1,0:T(4,128)S(1)}, f32[1024,1024,4]{1,0,2:T(8,128)S(1)}) fusion(pred[1024,1024]{0,1:T(8,128)(4,1)S(1)} %fusion.51, bf16[2,1,1024,4,128]{4,2,3,1,0:T(8,128)(2,1)} %get-tuple-element.153, s32[]{:T(128)} %get-tuple-element.142, bf16[2,1,1024,128]{2,3,0,1:T(8,128)(2,1)S(1)} %get-tuple-element.152), kind=kOutput, calls=%fused_computation.6.clone.1 | convolution fusion | flops 1086320640 | bytes 19153920 | tf_op jit(solution)/shard_map/while/body/eval_jaxpr/nigd,njd->ngij/dot_general | solution.py:84
  165.7 3.7 %fusion.53 = f32[4,1024]{1,0:T(4,128)S(1)} fusion(f32[1024,1024,4]{1,0,2:T(8,128)S(1)} %get-tuple-element.133, f32[4,1024]{1,0:T(4,128)S(1)} %get-tuple-element.134, pred[1024,1024]{0,1:T(8,128)(4,1)S(1)} %fusion.51), kind=kLoop, calls=%fused_computation.5.clone.1 | loop fusion | flops 16773120 | bytes 17858560 | tf_op jit(solution)/shard_map/while/body/eval_jaxpr/reduce_sum | solution.py:92
  169.3 6.2 %fusion.54 = bf16[2,1,1024,4,128]{2,4,3,1,0:T(8,128)(2,1)} fusion(bf16[2,1,1024,4,128]{2,4,3,1,0:T(8,128)(2,1)} %get-tuple-element.143, s32[]{:T(128)} %get-tuple-element.142, f32[4,1024]{1,0:T(4,128)S(1)} %fusion.53, f32[4,1024]{1,0:T(4,128)S(1)} %get-tuple-element.134, f32[1024,1024,4]{1,0,2:T(8,128)S(1)} %get-tuple-element.133, ...), kind=kOutput, calls=%fused_computation.14.clone.1 | convolution fusion | flops 1095237632 | bytes 19170304 | tf_op jit(solution)/shard_map/while/body/eval_jaxpr/ngij,njd->nigd/dot_general | solution.py:95
  175.5 16.1 %fusion.36 = f32[1024,4096]{1,0:T(8,128)} fusion(bf16[1024,1024]{0,1:T(8,128)(2,1)} %bitcast.21, bf16[1024,4096]{1,0:T(8,128)(2,1)} %param.17), kind=kOutput, calls=%fused_computation.59 | convolution fusion | flops 8589934592 | bytes 27262976 | tf_op jit(solution)/shard_map/dot_general | solution.py:115
  194.9 7.8 %all-to-all-start = ((bf16[32,32,512]{2,1,0:T(8,128)(2,1)}), bf16[32,32,512]{2,1,0:T(8,128)(2,1)}, u32[]{:S(2)}, u32[]{:S(2)}) async-start(bf16[32,32,512]{2,1,0:T(8,128)(2,1)} %reshape_squeeze_reshape.3), calls=%async_computation.1 | async-start | bytes 2097152 | tf_op jit(solution)/shard_map/all_to_all | solution.py:41
  202.8 16.8 %all-to-all-done = bf16[32,32,512]{2,1,0:T(8,128)(2,1)} async-done(((bf16[32,32,512]{2,1,0:T(8,128)(2,1)}), bf16[32,32,512]{2,1,0:T(8,128)(2,1)}, u32[]{:S(2)}, u32[]{:S(2)}) %all-to-all-start) | async-done | bytes 1048608 | tf_op jit(solution)/shard_map/all_to_all | solution.py:41
  221.7 20.6 %all_to_all.10 = bf16[32,32,512]{2,1,0:T(8,128)(2,1)S(1)} all-to-all(bf16[32,32,512]{2,1,0:T(8,128)(2,1)S(1)} %broadcast_select_fusion), channel_id=1, replica_groups=mesh['dp'=32,'ctx'=4] {'dp'}, dimensions={0} | all-to-all | bytes 2097152 | tf_op jit(solution)/shard_map/all_to_all | solution.py:43
  242.3 98.4 %reduce-scatter.2.cloned.1.call-done = f32[256,4096]{1,0:T(8,128)} async-done(((f32[1024,4096]{1,0:T(8,128)}), f32[256,4096]{1,0:T(8,128)}) %reduce-scatter.2.cloned.1.call-update) | async-done | bytes 4194320 | tf_op jit(solution)/shard_map/reduce_scatter | solution.py:114
  340.8 3.8 %convert_bitcast_fusion = bf16[1,256,4096]{2,1,0:T(8,128)(2,1)} fusion(f32[256,4096]{1,0:T(8,128)} %reduce-scatter.2.cloned.1.call-done), kind=kLoop, calls=%fused_computation.35 | loop fusion | flops 1048576 | bytes 6291456 | tf_op jit(solution)/shard_map/reshape | solution.py:120
  (54 shorter events, 17.0 us)
Async XLA Ops:
  7.2 132.8 %copy-start = (bf16[4096,256]{1,0:T(8,128)(2,1)S(1)}, bf16[4096,256]{1,0:T(8,128)(2,1)}, u32[]{:S(2)}) copy-start(bf16[4096,256]{1,0:T(8,128)(2,1)} %param.16) | copy-start | bytes 6291460
  7.2 88.9 %all-gather.5.cloned.1.call-start = ((), (), s32[]{:S(2)}) async-start(), calls=%async_computation.4 | async-start | bytes 10485760 | tf_op jit(solution)/shard_map/all_gather | solution.py:48
  7.9 332.9 %reduce-scatter.2.cloned.1.call-start = ((), (), s32[]{:S(2)}) async-start(), calls=%async_computation.3 | async-start | bytes 20971520 | tf_op jit(solution)/shard_map/reduce_scatter | solution.py:114
  12.1 11.6 %copy-start.9 = (s32[1,256]{1,0:T(1,128)S(1)}, s32[1,256]{1,0:T(1,128)}, u32[]{:S(2)}) copy-start(s32[1,256]{1,0:T(1,128)} %param.11) | copy-start | bytes 3076
  23.7 77.6 %copy-start.8 = (f32[4096]{0:T(1024)S(1)}, f32[4096]{0:T(1024)}, u32[]{:S(2)}) copy-start(f32[4096]{0:T(1024)} %param.13) | copy-start | bytes 49156
  35.0 80.5 %copy-start.6 = (f32[1024,64]{0,1:T(8,128)}, f32[1024,64]{0,1:T(8,128)S(1)}, u32[]{:S(2)}) copy-start(f32[1024,64]{0,1:T(8,128)S(1)} %get-tuple-element.92) | copy-start | bytes 786436
  35.0 80.5 %copy-start.7 = (f32[1024,64]{0,1:T(8,128)}, f32[1024,64]{0,1:T(8,128)S(1)}, u32[]{:S(2)}) copy-start(f32[1024,64]{0,1:T(8,128)S(1)} %get-tuple-element.93) | copy-start | bytes 786436
  96.0 5.8 %copy-start.2 = (bf16[4,256,4096]{2,1,0:T(8,128)(2,1)S(1)}, bf16[4,256,4096]{2,1,0:T(8,128)(2,1)}, u32[]{:S(2)}) copy-start(bf16[4,256,4096]{2,1,0:T(8,128)(2,1)} %all-gather.5.cloned.1.call-done) | copy-start | bytes 25165828
  96.0 10.4 %slice-start = ((s8[8388608]{0:T(1024)(128)(4,1)}), s8[4194304]{0:T(1024)(128)(4,1)S(1)}, s32[]{:S(2)}) async-start(s8[8388608]{0:T(1024)(128)(4,1)} %bitcast.134), calls=%async_computation.5 | async-start | bytes 8388608
  101.8 4.7 %slice-start.1 = ((s8[8388608]{0:T(1024)(128)(4,1)}), s8[4194304]{0:T(1024)(128)(4,1)S(1)}, s32[]{:S(2)}) async-start(s8[8388608]{0:T(1024)(128)(4,1)} %bitcast.134), calls=%async_computation.6 | async-start | bytes 8388608
  116.4 13.2 %copy-start.3 = (bf16[1,1024,2,64]{1,3,2,0:T(8,128)(2,1)}, bf16[1,1024,2,64]{1,3,2,0:T(8,128)(2,1)S(1)}, u32[]{:S(2)}) copy-start(bf16[1,1024,2,64]{1,3,2,0:T(8,128)(2,1)S(1)} %get-tuple-element.90) | copy-start | bytes 786436
  191.7 0.9 copy-start.4
  191.7 1.0 copy-start.5
  191.7 11.0 %copy-start.10 = (s32[32]{0:T(128)S(1)}, s32[32]{0:T(128)}, u32[]{:S(2)}) copy-start(s32[32]{0:T(128)} %param.12) | copy-start | bytes 388
  193.7 151.9 %copy-start.1 = (bf16[4096,256]{1,0:T(8,128)(2,1)S(1)}, bf16[4096,256]{1,0:T(8,128)(2,1)}, u32[]{:S(2)}) copy-start(bf16[4096,256]{1,0:T(8,128)(2,1)} %param.16) | copy-start | bytes 6291460
  194.9 24.7 %all-to-all-start = ((bf16[32,32,512]{2,1,0:T(8,128)(2,1)}), bf16[32,32,512]{2,1,0:T(8,128)(2,1)}, u32[]{:S(2)}, u32[]{:S(2)}) async-start(bf16[32,32,512]{2,1,0:T(8,128)(2,1)} %reshape_squeeze_reshape.3), calls=%async_computation.1 | async-start | bytes 2097152 | tf_op jit(solution)/shard_map/all_to_all | solution.py:41
Sparse Core Ops, SparseCore 0:
  9.7 86.3 all-gather.4
  191.8 148.8 reduce-scatter.1
